TPU v7x, 256 devices: a whole 4x4x8 slice. The times are simulated.
256 devices in a mesh: seq: 32 (over z, x_hi, core), tp: 8 (over y, x_lo).
Axes of the slice: x: 4 (x_hi: 2, x_lo: 2; x = x_hi * 2 + x_lo), y: 4, z: 8, core: 2. Of those that a mesh axis runs over, the one named last changes fastest.
Arguments:
- tokens: bfloat16 [12288, 4096], P('seq', 'tp'), may hold values from -6 to 6
- valid: int32 [96], P('seq'), may hold values from 1 to 128, as said below
- seg_query: bfloat16 [4096, 2048], P('seq', 'tp'), may hold values from -1 to 1
- seg_key: bfloat16 [4096, 2048], P('seq', 'tp'), may hold values from -1 to 1
- seg_value: bfloat16 [4096, 2048], P('seq', 'tp'), may hold values from -0.09375 to 0.09375
- seg_output: bfloat16 [2048, 4096], P('tp', 'seq'), may hold values from -0.125 to 0.125
- cross_query: bfloat16 [4096, 2048], P('seq', 'tp'), may hold values from -1 to 1
- cross_key: bfloat16 [4096, 2048], P('seq', 'tp'), may hold values from -1 to 1
- cross_value: bfloat16 [4096, 2048], P('seq', 'tp'), may hold values from -0.09375 to 0.09375
- cross_output: bfloat16 [2048, 4096], P('tp', 'seq'), may hold values from -0.125 to 0.125
- cotangent: bfloat16 [12288, 4096], P('seq', 'tp'), may hold values from -0.59765625 to 0.59765625
Outputs:
- layer_out: bfloat16 [12288, 4096], P('seq', 'tp')
- cross_update: float32 [96, 4096], P('seq', 'tp')
- cross_output_grad: float32 [2048, 4096], P('tp', 'seq')
Inputs may be any that keep to these rules, and one draw needn't show every extreme that they name: valid[s] counts the real tokens of segment s, the first being its summary token; segments wholly inside the document hold 64 to 128 tokens, segments after the document's end hold only the summary token.
All inputs are finite; a program needn't handle non-finite values.
Results may differ from a plain program's by a relative error of at most 0.024.
Values may be sent and summed in bfloat16 or wider, within the bound.
No kernel may reach another device: no remote copies, remote signals or barrier semaphores. Data moves between devices by JAX's collectives and lax.ppermute only.
A program may use at most 64 MiB of HBM per device.

v0:
```python
import jax
import jax.numpy as jnp
from jax import lax
from jax.experimental import pallas as pl
from jax.experimental.pallas import tpu as pltpu
from jax.sharding import PartitionSpec as P

HD = 128
SEG = 128
EPS = 1e-05
NZ = 8
NY = 4
BF = jnp.bfloat16
F32 = jnp.float32
VMEM = pl.BlockSpec(memory_space=pltpu.VMEM)
SMEM = pl.BlockSpec(memory_space=pltpu.SMEM)

CORE = [(i, i ^ 1) for i in range(32)]
XHI = [(i, i ^ 2) for i in range(32)]
XLO = [(i, i ^ 1) for i in range(8)]


def along_z(step):
    return [(i, (i + 4 * step) % 32) for i in range(32)]


def along_y(step):
    return [(i, (i + 2 * step) % 8) for i in range(8)]


def call(body, outs, args, scratch=(), flops=0, moved=0):
    specs = [SMEM if a.dtype == jnp.int32 else VMEM for a in args]
    return pl.pallas_call(
        body,
        out_shape=outs,
        in_specs=specs,
        out_specs=[VMEM] * len(outs),
        scratch_shapes=list(scratch),
        compiler_params=pltpu.CompilerParams(vmem_limit_bytes=16 * 2**20),
        cost_estimate=pl.CostEstimate(flops=flops, bytes_accessed=moved, transcendentals=0),
    )(*args)


def shape(dims, dtype):
    return jax.ShapeDtypeStruct(dims, dtype)


def dot(a, b):
    return jnp.dot(a, b, preferred_element_type=F32)


def tie(*arrays):
    return lax.optimization_barrier(arrays)


def in_order(flag, mine, other, axis):
    return jnp.concatenate(
        [jnp.where(flag, mine, other), jnp.where(flag, other, mine)], axis=axis
    )


def assemble_kernel(pos, p0, p1, p2a, p2b, p3, x_out, own_sq, sib_sq):
    core, y = pos[2], pos[3]
    rows = p0.shape[1]
    per = rows // 2
    x_out[0:2] = p0[...]
    x_out[2:4] = p1[...]
    x_out[4] = p2a[...]
    x_out[5] = p2b[...]
    x_out[6:8] = p3[...]
    segs = per // SEG
    for which, ref in ((0, own_sq), (1, sib_sq)):
        base = pl.multiple_of((core if which == 0 else 1 - core) * per, per)
        for j in range(segs):
            at = pl.ds(base + j * SEG, SEG)
            total = jnp.zeros((SEG, 128), F32)
            for k in range(8):
                v = x_out[k, at, :].astype(F32)
                total += v[:, :128] * v[:, :128] + v[:, 128:] * v[:, 128:]
            ref[j * SEG : (j + 1) * SEG, :] = jnp.broadcast_to(
                jnp.sum(total, axis=1, keepdims=True), (SEG, 128)
            )


def project_kernel(pos, x, *refs):
    w, (own, sib) = refs[:9], refs[9:]
    z, core, y = pos[0], pos[2], pos[3]
    per, width = own.shape
    half = w[4].shape[1]
    tile = SEG
    for which, ref in ((1, sib), (0, own)):
        base = pl.multiple_of((core if which == 0 else 1 - core) * per, per)
        for j in range(per // tile):
            at = pl.ds(base + j * tile, tile)
            total = None
            for k in range(8):
                index = lax.rem(z + k - 2 * y + 16, 8)
                rows = x[index, at, :]
                if k == 4:
                    term = jnp.concatenate(
                        [dot(rows, w[4][...]), dot(rows, w[5][:, : width - half])], axis=1
                    )
                else:
                    term = dot(rows, w[k if k < 4 else k + 1][:, :width])
                total = term if total is None else total + term
            ref[j * tile : (j + 1) * tile, :] = total.astype(ref.dtype)


def attend_kernel(valid, own, got, own_sq, got_sq, out, mixed):
    heads = mixed.shape[1] // HD
    width = heads * HD
    features = 4096.0
    for j in range(own.shape[0] // SEG):
        at = slice(j * SEG, (j + 1) * SEG)
        scale = lax.rsqrt((own_sq[at, :] + got_sq[at, :]) * (1.0 / features) + EPS)
        allowed = lax.broadcasted_iota(jnp.int32, (SEG, SEG), 1) < valid[j]
        for h in range(heads):
            parts = []
            for kind in range(3):
                cols = slice(kind * width + h * HD, kind * width + (h + 1) * HD)
                parts.append(((own[at, cols] + got[at, cols].astype(F32)) * scale).astype(BF))
            q, k, v = parts
            scores = lax.dot_general(
                q, k, (((1,), (1,)), ((), ())), preferred_element_type=F32
            ) * (HD**-0.5)
            scores = jnp.where(allowed, scores, -1e30)
            weights = jnp.exp(scores - jnp.max(scores, axis=1, keepdims=True))
            weights = (weights / jnp.sum(weights, axis=1, keepdims=True)).astype(BF)
            part = dot(weights, v).astype(BF)
            mixed[at, h * HD : (h + 1) * HD] = part
    for to in range(out.shape[0]):
        out[to] = mixed[...]


def out_kernel(pos, chip, own, sib, grads, *refs):
    w, (mine, theirs, summary, rows) = refs[:9], refs[9:]
    z, core = pos[0], pos[2]
    per = mine.shape[0]
    part = per // 2
    segs = per // SEG
    rows[...] = jnp.zeros_like(rows)
    for which, src, ref in ((0, own, mine), (1, sib, theirs)):
        chip_core = core if which == 0 else 1 - core
        for h in range(2):
            at = slice(h * part, (h + 1) * part)
            total = None
            for k in range(8):
                weights = w[k if k < 4 else k + 1]
                last = weights.shape[1]
                term = dot(src[lax.rem(z + k, 8), at, :], weights[:, last - 256 : last])
                total = term if total is None else total + term
            base = pl.multiple_of(chip_core * per + h * part, part)
            sums = (chip[pl.ds(base, part), :].astype(F32) + total).astype(BF)
            ref[at, :] = sums
            for j in range(segs):
                place = j * SEG - h * part
                if 0 <= place < part:
                    row = sums[place : place + 16, :].astype(F32)[0:1]
                    rows[pl.ds(chip_core * segs + j, 1), :] = row
    for to in range(summary.shape[0]):
        summary[to, 0:8, :] = rows[...]
        summary[to, 8:16, :] = grads[...]


def cross_project_kernel(pos, rows, *refs):
    w, out, table = refs[:9], refs[9], refs[10]
    z = pos[0]
    width = out.shape[1] - 128
    half = w[4].shape[1]
    total = jnp.zeros((8, width), F32)
    square = jnp.zeros((8, 128), F32)
    for k in range(8):
        at = lax.rem(z + k, 8)
        wide = rows[at, 0:8, :]
        ref = w[k if k < 4 else k + 1]
        table[at] = ref[:, ref.shape[1] - 512 : ref.shape[1] - 256]
        square += wide[:, :128] * wide[:, :128] + wide[:, 128:] * wide[:, 128:]
        wide = wide.astype(BF)
        if k == 4:
            total += jnp.concatenate(
                [dot(wide, w[4][...]), dot(wide, w[5][:, : width - half])], axis=1
            )
        else:
            total += dot(wide, ref[:, :width])
    out[:, :width] = total
    out[:, width:] = jnp.broadcast_to(jnp.sum(square, axis=1, keepdims=True), (8, 128))


def cross_scale_kernel(own, got, out):
    width = own.shape[1] - 128
    scale = lax.rsqrt((own[:, width:] + got[:, width:]) * (1.0 / 4096.0) + EPS)
    for k in range(width // 128):
        cols = slice(k * 128, (k + 1) * 128)
        block = ((own[:, cols] + got[:, cols]) * scale).astype(BF)
        for to in range(out.shape[0]):
            out[to, :, cols] = block


def cross_attend_kernel(pos, gathered, w, mixed, update, table):
    z, x_hi = pos[0], pos[1]
    count = gathered.shape[0] * 8
    rows = gathered[...].astype(F32).reshape(count, gathered.shape[2]).astype(BF)
    width = rows.shape[1] // 3
    key_index = lax.broadcasted_iota(jnp.int32, (count, count), 1)
    allowed = key_index % 8 < 6
    for h in range(width // HD):
        q = rows[:, h * HD : (h + 1) * HD]
        k = rows[:, width + h * HD : width + (h + 1) * HD]
        v = rows[:, 2 * width + h * HD : 2 * width + (h + 1) * HD]
        scores = lax.dot_general(
            q, k, (((1,), (1,)), ((), ())), preferred_element_type=F32
        ) * (HD**-0.5)
        scores = jnp.where(allowed, scores, -1e30)
        weights = jnp.exp(scores - jnp.max(scores, axis=1, keepdims=True))
        weights = (weights / jnp.sum(weights, axis=1, keepdims=True)).astype(BF)
        table[:, h * HD : (h + 1) * HD] = dot(weights, v)
    mixed[...] = table[...].astype(BF)
    chip = table[pl.ds(pl.multiple_of((z * 2 + x_hi) * 8, 8), 8), :].astype(BF)
    for k in range(8):
        update[k] = dot(chip, w[k])


def update_kernel(pos, parts, mine, theirs):
    core = pos[2]
    total = parts[0]
    for k in range(1, parts.shape[0]):
        total = total + parts[k]
    later = jnp.concatenate([total[3:], total[:3]], axis=0)
    mine[...] = jnp.where(core == 0, total, later)
    theirs[...] = jnp.where(core == 0, later, total)


def final_kernel(pos, valid, seg_mine, seg_theirs, mine, theirs, out, update):
    core = pos[2]
    segs = update.shape[0]
    place = lax.broadcasted_iota(jnp.int32, (SEG, 1), 0)
    for which, seg, ref in ((0, seg_mine, mine), (1, seg_theirs, theirs)):
        part = core if which == 0 else 1 - core
        for x in range(2):
            cols = pl.ds(pl.multiple_of(x * 256 + part * 128, 128), 128)
            from_cols = slice(x * 128, (x + 1) * 128)
            update[:, cols] = ref[:segs, from_cols]
            for j in range(segs):
                at = slice(j * SEG, (j + 1) * SEG)
                live = (place < valid[j]).astype(F32)
                sums = seg[at, from_cols].astype(F32) + ref[j : j + 1, from_cols]
                out[at, cols] = (sums * live).astype(BF)


def grad_kernel(mixed, grads, out):
    total = jnp.zeros(out.shape, F32)
    for k in range(8):
        block = grads[k, 8:16, :]
        right = jnp.concatenate([block[:, :128], block[:, 128:]], axis=0).astype(BF)
        total += lax.dot_general(
            mixed[k * 16 : (k + 1) * 16, :], right, (((0,), (0,)), ((), ())),
            preferred_element_type=F32,
        )
    out[...] = total


def local(
    tokens, valid, seg_query, seg_key, seg_value, seg_output,
    cross_query, cross_key, cross_value, cross_output, cotangent,
):
    per, cols = tokens.shape
    segs = per // SEG
    s = lax.axis_index("seq")
    t = lax.axis_index("tp")
    z, x_hi, core = s // 4, (s // 2) % 2, s % 2
    y, x_lo = t // 2, t % 2
    pos = jnp.stack([z, x_hi, core, y, x_lo]).astype(jnp.int32)
    is0 = core == 0

    at0 = x_hi == 0
    low = x_lo == 0
    swap = [
        (i * 8 + j, (j * 4 + i % 4) * 8 + i // 4) for i in range(32) for j in range(8)
    ]


    def z_step(block, step):
        return lax.ppermute(block, "seq", along_z(step))

    def y_step(block, step):
        return lax.ppermute(block, "tp", along_y(step))

    four = tokens.reshape(per, 2, 2, 128)
    keep = jnp.where(is0, four[:, :, 0], four[:, :, 1]).reshape(per, 256)
    give = jnp.where(is0, four[:, :, 1], four[:, :, 0]).reshape(per, 256)
    block = jnp.concatenate([seg_query, seg_key, seg_value], axis=1)
    cross_block = jnp.concatenate([cross_query, cross_key, cross_value], axis=1)
    far = lax.ppermute(block, "seq", XHI)
    take = lax.ppermute(give, "seq", CORE)
    live = jnp.arange(SEG, dtype=jnp.int32)[None, :] < valid[:, None]
    keep_rows = live.astype(F32)[:, :, None]
    grad = jnp.sum(cotangent.astype(F32).reshape(segs, SEG, cols) * keep_rows, axis=1)
    grad = jnp.pad(grad.astype(BF), ((0, 1), (0, 0))).reshape(16, 128)
    turned = lax.ppermute(jnp.concatenate([seg_output, grad], axis=0), ("seq", "tp"), swap)
    far, take = tie(far, take)

    plane = in_order(at0, block, far, 0)
    chip = in_order(is0, keep, take, 0)
    chip_x = lax.ppermute(chip, "tp", XLO)
    up1, down1 = z_step(plane, 1), z_step(plane, -1)
    up1, down1, chip_x, turned, cross_block, cross_output = tie(
        up1, down1, chip_x, turned, cross_block, cross_output
    )

    up2, down2 = z_step(up1, 1), z_step(down1, -1)
    p0 = in_order(low, chip[None], chip_x[None], 0)
    p3, p1 = y_step(p0, 1), y_step(p0, -1)
    grad = turned[256:].reshape(segs + 1, 2, 2, 128)[:segs]
    g_keep = jnp.where(is0, grad[:, :, 0], grad[:, :, 1])
    g_take = lax.ppermute(jnp.where(is0, grad[:, :, 1], grad[:, :, 0]), "seq", CORE)
    cross_pack = jnp.concatenate(
        [cross_block, cross_output[:128], cross_output[128:], turned[:128], turned[128:256]],
        axis=1,
    )
    cross_far = lax.ppermute(cross_pack, "seq", XHI)
    up2, down2, cross_far, g_take = tie(up2, down2, cross_far, g_take)

    up3, down3 = z_step(up2, 1), z_step(down2, -1)
    g_chip = jnp.concatenate(
        [in_order(is0, g_keep, g_take, 0), jnp.zeros((8 - 2 * segs, 2, 128), BF)]
    )
    g_own = jnp.where(at0, g_chip[:, 0], g_chip[:, 1])
    g_far = lax.ppermute(jnp.where(at0, g_chip[:, 1], g_chip[:, 0]), "seq", XHI)
    g_rows = in_order(at0, g_own, g_far, 1).astype(F32)

    def tall(wide):
        return jnp.concatenate([wide[:, :128], wide[:, 128:]], axis=0)

    cross_plane = jnp.concatenate(
        [
            in_order(at0, cross_block, cross_far[:, :768], 0),
            in_order(at0, cross_output, tall(cross_far[:, 768:1024]), 1),
            in_order(at0, turned[:256], tall(cross_far[:, 1024:]), 1),
        ],
        axis=1,
    )
    up3, down3, cross_plane, g_rows = tie(up3, down3, cross_plane, g_rows)

    half = plane.shape[1] // 2
    up4, down4 = z_step(up3[:, :half], 1), z_step(down3[:, half:], -1)
    p2a, p2b = y_step(p3[0], 1), y_step(p1[1], -1)
    p2a, cross_plane = tie(p2a, cross_plane)
    c_up1, c_down1 = z_step(cross_plane, 1), z_step(cross_plane, -1)
    up4, down4, p2a, p2b = tie(up4, down4, p2a, p2b)

    x, own_sq, sib_sq = call(
        assemble_kernel,
        [shape((8, 2 * per, 256), BF), shape((per, 128), F32), shape((per, 128), F32)],
        (pos, p0, p1, p2a, p2b, p3),
        moved=8 * 2**20,
    )
    got_sq = lax.ppermute(sib_sq, "seq", CORE)
    own_p, sib_p = call(
        project_kernel,
        [shape((per, 768), F32), shape((per, 768), BF)],
        (pos, x, plane, down1, down2, down3, up4, down4, up3, up2, up1),
        flops=2 * 768 * 768 * 2048,
        moved=8 * 2**20,
    )
    got_p = lax.ppermute(sib_p, "seq", CORE)
    got_p, got_sq, c_up1, c_down1 = tie(got_p, got_sq, c_up1, c_down1)
    c_up2, c_down2 = z_step(c_up1, 1), z_step(c_down1, -1)
    (mixed,) = call(
        attend_kernel,
        [shape((8, per, 256), BF)],
        (valid, own_p, got_p, own_sq, got_sq),
        scratch=[pltpu.VMEM((per, 256), BF)],
        flops=10**8,
        moved=3 * 2**20,
    )

    mixed, c_up2, c_down2 = tie(mixed, c_up2, c_down2)
    c_up3, c_down3 = z_step(c_up2, 1), z_step(c_down2, -1)
    mixed = lax.all_to_all(mixed, "tp", 0, 0)
    mixed, c_up3, c_down3 = tie(mixed, c_up3, c_down3)
    half = cross_plane.shape[1] // 2
    c_up4, c_down4 = z_step(c_up3[:, :half], 1), z_step(c_down3[:, half:], -1)
    cross_w = (
        cross_plane, c_down1, c_down2, c_down3, c_up4, c_down4, c_up3, c_up2, c_up1
    )
    mixed_sib = lax.ppermute(mixed, "seq", CORE)
    seg_mine, seg_give, summary = call(
        out_kernel,
        [shape((per, 256), BF), shape((per, 256), BF), shape((8, 16, 256), F32)],
        (pos, chip, mixed, mixed_sib, g_rows, *cross_w),
        scratch=[pltpu.VMEM((8, 256), F32)],
        flops=2 * per * 512 * 2048,
        moved=6 * 2**20,
    )
    summaries = lax.all_to_all(summary, "tp", 0, 0)
    seg_take = lax.ppermute(seg_give, "seq", CORE)

    cross_part, back_w = call(
        cross_project_kernel,
        [shape((8, 896), F32), shape((8, 256, 256), BF)],
        (pos, summaries, *cross_w),
        flops=10**8,
        moved=3 * 2**20,
    )
    cross_got = lax.ppermute(cross_part, "seq", CORE)
    (rows,) = call(
        cross_scale_kernel, [shape((16, 8, 768), BF)], (cross_part, cross_got), moved=10**6
    )
    same_core = [[i * 2 + k for i in range(16)] for k in range(2)]
    gathered = lax.all_to_all(rows, "seq", 0, 0, axis_index_groups=same_core)
    cross_mixed, update = call(
        cross_attend_kernel,
        [shape((128, 256), BF), shape((8, 8, 256), F32)],
        (pos, gathered, back_w),
        scratch=[pltpu.VMEM((128, 256), F32)],
        flops=10**8,
        moved=10**6,
    )
    parts = lax.all_to_all(update, "tp", 0, 0)
    mine, theirs = call(
        update_kernel, [shape((8, 256), F32), shape((8, 256), F32)], (pos, parts), moved=10**5
    )
    got_update = lax.ppermute(theirs, "seq", CORE)
    layer_out, cross_update = call(
        final_kernel,
        [shape((per, cols), BF), shape((segs, cols), F32)],
        (pos, valid, seg_mine, seg_take, mine, got_update),
        flops=10**6,
        moved=10**6,
    )
    (grad_weight,) = call(
        grad_kernel,
        [shape((256, 128), F32)],
        (cross_mixed, summaries),
        flops=10**7,
        moved=10**5,
    )
    return (layer_out, cross_update, grad_weight)


def solution(mesh):
    return jax.shard_map(
        local,
        mesh=mesh,
        in_specs=(
            P("seq", "tp"),
            P("seq"),
            P("seq", "tp"),
            P("seq", "tp"),
            P("seq", "tp"),
            P("tp", "seq"),
            P("seq", "tp"),
            P("seq", "tp"),
            P("seq", "tp"),
            P("tp", "seq"),
            P("seq", "tp"),
        ),
        out_specs=(P("seq", "tp"), P("seq", "tp"), P("tp", "seq")),
        check_vma=False,
    )
```

profile of v0, /device:TPU:1, one launch (start us, length us, event | category | flops | bytes accessed | tf_op | source)
XLA Modules:
  0.0 190.1 jit_solution(9900496466716350206)
XLA Ops:
  2.8 3.3 %collective-permute-start.1 = (bf16[384,256]{1,0:T(8,128)(2,1)S(1)}, bf16[384,256]{1,0:T(8,128)(2,1)S(1)}, u32[]{:S(2)}, u32[]{:S(2)}) collective-permute-start(bf16[384,256]{1,0:T(8,128)(2,1)S(1)} %bitcast.40), channel_id=1, source_target_pairs={{0,8},{8,0},{16,24},{24,16},{32,40},{40,32},{48,56},{56,48},{64,72... | collective-permute-start | bytes 589832 | tf_op jit(solution)/shard_map/ppermute | solution.py:294
  7.3 7.0 %collective-permute-done = bf16[128,768]{1,0:T(8,128)(2,1)S(1)} collective-permute-done((bf16[128,768]{1,0:T(8,128)(2,1)S(1)}, bf16[128,768]{1,0:T(8,128)(2,1)S(1)}, u32[]{:S(2)}, u32[]{:S(2)}) %collective-permute-start) | collective-permute-done | bytes 196640 | tf_op jit(solution)/shard_map/ppermute | solution.py:293
  14.5 3.9 %collective-permute-start.3 = (bf16[256,768]{1,0:T(8,128)(2,1)S(1)}, bf16[256,768]{1,0:T(8,128)(2,1)}, u32[]{:S(2)}, u32[]{:S(2)}) collective-permute-start(bf16[256,768]{1,0:T(8,128)(2,1)S(1)} %pad_maximum_fusion.2.refs_0_), channel_id=1, source_target_pairs={{0,224},{8,232},{16,240},{24,248},{32,0},{40,8},{48,16},{56,24},{6... | collective-permute-start | bytes 1179656 | tf_op jit(solution)/shard_map/ppermute | solution.py:283
  21.4 5.6 %collective-permute-done.2.refs_8_ = bf16[256,768]{1,0:T(8,128)(2,1)S(1)} collective-permute-done((bf16[256,768]{1,0:T(8,128)(2,1)S(1)}, bf16[256,768]{1,0:T(8,128)(2,1)S(1)}, u32[]{:S(2)}, u32[]{:S(2)}) %collective-permute-start.2) | collective-permute-done | bytes 393248 | tf_op jit(solution)/shard_map/ppermute | solution.py:283
  27.0 5.4 %collective-permute-done.4 = bf16[768,256]{1,0:T(8,128)(2,1)S(1)} collective-permute-done((bf16[768,256]{1,0:T(8,128)(2,1)S(1)}, bf16[768,256]{1,0:T(8,128)(2,1)S(1)}, u32[]{:S(2)}, u32[]{:S(2)}) %collective-permute-start.4) | collective-permute-done | bytes 393248 | tf_op jit(solution)/shard_map/ppermute | solution.py:304
  32.5 2.7 %collective-permute-start.10 = (bf16[3,2,128]{2,0,1:T(4,128)(2,1)S(1)}, bf16[3,2,128]{2,0,1:T(4,128)(2,1)S(1)}, u32[]{:S(2)}, u32[]{:S(2)}) collective-permute-start(bf16[3,2,128]{2,0,1:T(4,128)(2,1)S(1)} %select_bitcast_fusion.3), channel_id=1, source_target_pairs={{0,8},{8,0},{16,24},{24,16},{32,40},{40,32},{48,56},{56,48},{64,72... | collective-permute-start | bytes 4616 | tf_op jit(solution)/shard_map/ppermute | solution.py:315
  35.4 5.5 %collective-permute-start.8 = (bf16[256,768]{1,0:T(8,128)(2,1)}, bf16[256,768]{1,0:T(8,128)(2,1)S(1)}, u32[]{:S(2)}, u32[]{:S(2)}) collective-permute-start(bf16[256,768]{1,0:T(8,128)(2,1)} %collective-permute-done.3.refs_1_), channel_id=1, source_target_pairs={{0,224},{8,232},{16,240},{24,248},{32,0},{40,8},{48,16},{56,24},{6... | collective-permute-start | bytes 1179656 | tf_op jit(solution)/shard_map/ppermute | solution.py:283
  46.5 5.0 %collective-permute-done.9 = bf16[128,1280]{1,0:T(8,128)(2,1)S(1)} collective-permute-done((bf16[128,1280]{1,0:T(8,128)(2,1)S(1)}, bf16[128,1280]{1,0:T(8,128)(2,1)S(1)}, u32[]{:S(2)}, u32[]{:S(2)}) %collective-permute-start.9) | collective-permute-done | bytes 327712 | tf_op jit(solution)/shard_map/ppermute | solution.py:320
  57.1 6.4 %collective-permute-done.16.p3 = bf16[2,768,256]{2,1,0:T(8,128)(2,1)S(1)} collective-permute-done((bf16[2,768,256]{2,1,0:T(8,128)(2,1)S(1)}, bf16[2,768,256]{2,1,0:T(8,128)(2,1)S(1)}, u32[]{:S(2)}, u32[]{:S(2)}) %collective-permute-start.16) | collective-permute-done | bytes 786464 | tf_op jit(solution)/shard_map/ppermute | solution.py:286
  75.0 2.7 %collective-permute-start.22 = (bf16[256,1280]{1,0:T(8,128)(2,1)S(1)}, bf16[256,1280]{1,0:T(8,128)(2,1)S(1)}, u32[]{:S(2)}, u32[]{:S(2)}) collective-permute-start(bf16[256,1280]{1,0:T(8,128)(2,1)S(1)} %select_dynamic-update-slice_fusion.refs_0_), channel_id=1, source_target_pairs={{0,224},{8,232},{16,240},{24,248},{32,0},{40,8},{48,16},{56,24},{6... | collective-permute-start | bytes 1966088 | tf_op jit(solution)/shard_map/ppermute | solution.py:283
  81.0 4.0 %shard_map.131 = (f32[384,768]{1,0:T(8,128)S(1)}, bf16[384,768]{1,0:T(8,128)(2,1)S(1)}) custom-call(s32[5]{0:T(128)S(1)} %stack.23.pos, bf16[8,768,256]{2,1,0:T(8,128)(2,1)S(1)} %get-tuple-element.69.x, bf16[256,768]{1,0:T(8,128)(2,1)S(1)} %pad_maximum_fusion.2.refs_0_, bf16[256,768]{1,0:T(8,128)(2,1)} %collective-permute-done.3.refs_1_, ...), custom_call_target="tpu_custom_call" | custom-call | flops 2415919104 | bytes 8388608 | tf_op jit(solution)/shard_map/pallas_call | solution.py:33
  85.0 3.0 %collective-permute-start.19 = (bf16[384,768]{1,0:T(8,128)(2,1)S(1)}, bf16[384,768]{1,0:T(8,128)(2,1)S(1)}, u32[]{:S(2)}, u32[]{:S(2)}) collective-permute-start(bf16[384,768]{1,0:T(8,128)(2,1)S(1)} %get-tuple-element.73), channel_id=1, source_target_pairs={{0,8},{8,0},{16,24},{24,16},{32,40},{40,32},{48,56},{56,48},{64,72... | collective-permute-start | bytes 1769480 | tf_op jit(solution)/shard_map/ppermute | solution.py:365
  92.8 3.8 %shard_map.132 = bf16[8,384,256]{2,1,0:T(8,128)(2,1)} custom-call(s32[3]{0:T(128)S(1)} %copy-done.14, f32[384,768]{1,0:T(8,128)S(1)} %get-tuple-element.72.own, bf16[384,768]{1,0:T(8,128)(2,1)S(1)} %collective-permute-done.19.got, f32[384,128]{1,0:T(8,128)S(1)} %get-tuple-element.77.own_sq, f32[384,128]{1,0:T(8,128)S(1)} %collective-permute-done.20.got_sq), custom_call_target="tpu_custom_call" | custom-call | flops 100000000 | bytes 3145728 | tf_op jit(solution)/shard_map/pallas_call | solution.py:33
  96.7 7.7 %collective-permute-done.23.refs_7_ = bf16[256,1280]{1,0:T(8,128)(2,1)} collective-permute-done((bf16[256,1280]{1,0:T(8,128)(2,1)S(1)}, bf16[256,1280]{1,0:T(8,128)(2,1)}, u32[]{:S(2)}, u32[]{:S(2)}) %collective-permute-start.23) | collective-permute-done | bytes 655392 | tf_op jit(solution)/shard_map/ppermute | solution.py:283
  104.4 3.6 %all-to-all-start = ((bf16[8,384,256]{2,1,0:T(8,128)(2,1)}), bf16[8,384,256]{2,1,0:T(8,128)(2,1)S(1)}, u32[]{:S(2)}, u32[]{:S(2)}) async-start(bf16[8,384,256]{2,1,0:T(8,128)(2,1)} %shard_map.132), calls=%async_computation | async-start | bytes 3145728 | tf_op jit(solution)/shard_map/all_to_all | solution.py:379
  111.0 10.8 %collective-permute-done.25.refs_6_ = bf16[256,1280]{1,0:T(8,128)(2,1)S(1)} collective-permute-done((bf16[256,1280]{1,0:T(8,128)(2,1)}, bf16[256,1280]{1,0:T(8,128)(2,1)S(1)}, u32[]{:S(2)}, u32[]{:S(2)}) %collective-permute-start.25) | collective-permute-done | bytes 655392 | tf_op jit(solution)/shard_map/ppermute | solution.py:283
  121.8 3.4 %all-to-all-done.own = bf16[8,384,256]{2,1,0:T(8,128)(2,1)S(1)} async-done(((bf16[8,384,256]{2,1,0:T(8,128)(2,1)}), bf16[8,384,256]{2,1,0:T(8,128)(2,1)S(1)}, u32[]{:S(2)}, u32[]{:S(2)}) %all-to-all-start) | async-done | bytes 1572896 | tf_op jit(solution)/shard_map/all_to_all | solution.py:379
  125.2 5.1 %collective-permute-start.27 = (bf16[8,384,256]{2,1,0:T(8,128)(2,1)S(1)}, bf16[8,384,256]{2,1,0:T(8,128)(2,1)S(1)}, u32[]{:S(2)}, u32[]{:S(2)}) collective-permute-start(bf16[8,384,256]{2,1,0:T(8,128)(2,1)S(1)} %all-to-all-done.own), channel_id=1, source_target_pairs={{0,8},{8,0},{16,24},{24,16},{32,40},{40,32},{48,56},{56,48},{64,72... | collective-permute-start | bytes 4718600 | tf_op jit(solution)/shard_map/ppermute | solution.py:386
  133.2 7.8 %collective-permute-done.28.refs_4_ = bf16[256,640]{1,0:T(8,128)(2,1)S(1)} collective-permute-done((bf16[256,640]{1,0:T(8,128)(2,1)S(1)}, bf16[256,640]{1,0:T(8,128)(2,1)S(1)}, u32[]{:S(2)}, u32[]{:S(2)}) %collective-permute-start.28) | collective-permute-done | bytes 327712 | tf_op jit(solution)/shard_map/ppermute | solution.py:283
  145.0 8.0 %all_to_all.20.rows.grads = f32[8,16,256]{2,1,0:T(8,128)S(1)} all-to-all(f32[8,16,256]{2,1,0:T(8,128)S(1)} %get-tuple-element.90), channel_id=1, replica_groups=mesh['seq'=32,'tp'=8] {'tp'}, dimensions={0} | all-to-all | bytes 262144 | tf_op jit(solution)/shard_map/all_to_all | solution.py:395
  158.5 5.0 %all-to-all-start.2 = ((bf16[16,8,768]{2,1,0:T(8,128)(2,1)}), bf16[16,8,768]{2,1,0:T(8,128)(2,1)S(1)}, u32[]{:S(2)}, u32[]{:S(2)}) async-start(bf16[16,8,768]{2,1,0:T(8,128)(2,1)} %shard_map.135), calls=%async_computation.2 | async-start | bytes 393216 | tf_op jit(solution)/shard_map/all_to_all | solution.py:410
  164.2 10.4 %all-to-all-done.2.gathered = bf16[16,8,768]{2,1,0:T(8,128)(2,1)S(1)} async-done(((bf16[16,8,768]{2,1,0:T(8,128)(2,1)}), bf16[16,8,768]{2,1,0:T(8,128)(2,1)S(1)}, u32[]{:S(2)}, u32[]{:S(2)}) %all-to-all-start.2) | async-done | bytes 196640 | tf_op jit(solution)/shard_map/all_to_all | solution.py:410
  176.2 7.6 %all_to_all.21.parts = f32[8,8,256]{2,1,0:T(8,128)S(1)} all-to-all(f32[8,8,256]{2,1,0:T(8,128)S(1)} %get-tuple-element.93), channel_id=1, replica_groups=mesh['seq'=32,'tp'=8] {'tp'}, dimensions={0} | all-to-all | bytes 131072 | tf_op jit(solution)/shard_map/all_to_all | solution.py:419
  184.3 3.3 %collective-permute-start.32 = (f32[8,256]{1,0:T(8,128)S(1)}, f32[8,256]{1,0:T(8,128)S(1)}, u32[]{:S(2)}, u32[]{:S(2)}) collective-permute-start(f32[8,256]{1,0:T(8,128)S(1)} %get-tuple-element.95), channel_id=1, source_target_pairs={{0,8},{8,0},{16,24},{24,16},{32,40},{40,32},{48,56},{56,48},{64,72... | collective-permute-start | bytes 24584 | tf_op jit(solution)/shard_map/ppermute | solution.py:423
  (171 shorter events, 57.7 us)
Async XLA Ops:
  14.4 12.6 %collective-permute-start.2 = (bf16[256,768]{1,0:T(8,128)(2,1)S(1)}, bf16[256,768]{1,0:T(8,128)(2,1)S(1)}, u32[]{:S(2)}, u32[]{:S(2)}) collective-permute-start(bf16[256,768]{1,0:T(8,128)(2,1)S(1)} %pad_maximum_fusion.2.refs_0_), channel_id=1, source_target_pairs={{0,32},{8,40},{16,48},{24,56},{32,64},{40,72},{48,80},{56,88},{64,... | collective-permute-start | bytes 1179656 | tf_op jit(solution)/shard_map/ppermute | solution.py:283
  14.5 12.5 %collective-permute-start.3 = (bf16[256,768]{1,0:T(8,128)(2,1)S(1)}, bf16[256,768]{1,0:T(8,128)(2,1)}, u32[]{:S(2)}, u32[]{:S(2)}) collective-permute-start(bf16[256,768]{1,0:T(8,128)(2,1)S(1)} %pad_maximum_fusion.2.refs_0_), channel_id=1, source_target_pairs={{0,224},{8,232},{16,240},{24,248},{32,0},{40,8},{48,16},{56,24},{6... | collective-permute-start | bytes 1179656 | tf_op jit(solution)/shard_map/ppermute | solution.py:283
  18.5 14.0 %collective-permute-start.4 = (bf16[768,256]{1,0:T(8,128)(2,1)S(1)}, bf16[768,256]{1,0:T(8,128)(2,1)S(1)}, u32[]{:S(2)}, u32[]{:S(2)}) collective-permute-start(bf16[768,256]{1,0:T(8,128)(2,1)S(1)} %pad_maximum_fusion.1.chip), channel_id=1, source_target_pairs={{0,1},{1,0},{2,3},{3,2},{4,5},{5,4},{6,7},{7,6},{8,9},{9,8},{10,11... | collective-permute-start | bytes 1179656 | tf_op jit(solution)/shard_map/ppermute | solution.py:304
  32.5 11.3 %collective-permute-start.10 = (bf16[3,2,128]{2,0,1:T(4,128)(2,1)S(1)}, bf16[3,2,128]{2,0,1:T(4,128)(2,1)S(1)}, u32[]{:S(2)}, u32[]{:S(2)}) collective-permute-start(bf16[3,2,128]{2,0,1:T(4,128)(2,1)S(1)} %select_bitcast_fusion.3), channel_id=1, source_target_pairs={{0,8},{8,0},{16,24},{24,16},{32,40},{40,32},{48,56},{56,48},{64,72... | collective-permute-start | bytes 4616 | tf_op jit(solution)/shard_map/ppermute | solution.py:315
  35.3 16.2 %collective-permute-start.7 = (bf16[256,768]{1,0:T(8,128)(2,1)S(1)}, bf16[256,768]{1,0:T(8,128)(2,1)S(1)}, u32[]{:S(2)}, u32[]{:S(2)}) collective-permute-start(bf16[256,768]{1,0:T(8,128)(2,1)S(1)} %collective-permute-done.2.refs_8_), channel_id=1, source_target_pairs={{0,32},{8,40},{16,48},{24,56},{32,64},{40,72},{48,80},{56,88},{64,... | collective-permute-start | bytes 1179656 | tf_op jit(solution)/shard_map/ppermute | solution.py:283
  35.4 16.1 %collective-permute-start.8 = (bf16[256,768]{1,0:T(8,128)(2,1)}, bf16[256,768]{1,0:T(8,128)(2,1)S(1)}, u32[]{:S(2)}, u32[]{:S(2)}) collective-permute-start(bf16[256,768]{1,0:T(8,128)(2,1)} %collective-permute-done.3.refs_1_), channel_id=1, source_target_pairs={{0,224},{8,232},{16,240},{24,248},{32,0},{40,8},{48,16},{56,24},{6... | collective-permute-start | bytes 1179656 | tf_op jit(solution)/shard_map/ppermute | solution.py:283
  43.7 19.8 %collective-permute-start.16 = (bf16[2,768,256]{2,1,0:T(8,128)(2,1)S(1)}, bf16[2,768,256]{2,1,0:T(8,128)(2,1)S(1)}, u32[]{:S(2)}, u32[]{:S(2)}) collective-permute-start(bf16[2,768,256]{2,1,0:T(8,128)(2,1)S(1)} %pad_maximum_fusion.p0), channel_id=1, source_target_pairs={{0,2},{1,3},{2,4},{3,5},{4,6},{5,7},{6,0},{7,1},{8,10},{9,11},{10,... | collective-permute-start | bytes 2359304 | tf_op jit(solution)/shard_map/ppermute | solution.py:286
  43.8 20.5 %collective-permute-start.6 = (bf16[2,768,256]{2,1,0:T(8,128)(2,1)S(1)}, bf16[2,768,256]{2,1,0:T(8,128)(2,1)S(1)}, u32[]{:S(2)}, u32[]{:S(2)}) collective-permute-start(bf16[2,768,256]{2,1,0:T(8,128)(2,1)S(1)} %pad_maximum_fusion.p0), channel_id=1, source_target_pairs={{0,6},{1,7},{2,0},{3,1},{4,2},{5,3},{6,4},{7,5},{8,14},{9,15},{10,... | collective-permute-start | bytes 2359304 | tf_op jit(solution)/shard_map/ppermute | solution.py:286
  51.7 16.1 %collective-permute-start.13 = (bf16[8,128]{1,0:T(8,128)(2,1)S(1)}, bf16[8,128]{1,0:T(8,128)(2,1)S(1)}, u32[]{:S(2)}, u32[]{:S(2)}) collective-permute-start(bf16[8,128]{1,0:T(8,128)(2,1)S(1)} %select_bitcast_fusion.2), channel_id=1, source_target_pairs={{0,16},{8,24},{16,0},{24,8},{32,48},{40,56},{48,32},{56,40},{64,80... | collective-permute-start | bytes 6152 | tf_op jit(solution)/shard_map/ppermute | solution.py:328
  54.3 13.5 %collective-permute-start.11 = (bf16[256,768]{1,0:T(8,128)(2,1)S(1)}, bf16[256,768]{1,0:T(8,128)(2,1)S(1)}, u32[]{:S(2)}, u32[]{:S(2)}) collective-permute-start(bf16[256,768]{1,0:T(8,128)(2,1)S(1)} %collective-permute-done.7.refs_7_), channel_id=1, source_target_pairs={{0,32},{8,40},{16,48},{24,56},{32,64},{40,72},{48,80},{56,88},{64,... | collective-permute-start | bytes 1179656 | tf_op jit(solution)/shard_map/ppermute | solution.py:283
  54.4 13.5 %collective-permute-start.12 = (bf16[256,768]{1,0:T(8,128)(2,1)S(1)}, bf16[256,768]{1,0:T(8,128)(2,1)S(1)}, u32[]{:S(2)}, u32[]{:S(2)}) collective-permute-start(bf16[256,768]{1,0:T(8,128)(2,1)S(1)} %collective-permute-done.8.refs_2_), channel_id=1, source_target_pairs={{0,224},{8,232},{16,240},{24,248},{32,0},{40,8},{48,16},{56,24},{6... | collective-permute-start | bytes 1179656 | tf_op jit(solution)/shard_map/ppermute | solution.py:283
  64.3 10.7 %collective-permute-start.17 = (bf16[768,256]{1,0:T(8,128)(2,1)}, bf16[768,256]{1,0:T(8,128)(2,1)}, u32[]{:S(2)}, u32[]{:S(2)}) collective-permute-start(bf16[768,256]{1,0:T(8,128)(2,1)} %slice_bitcast_fusion.1), channel_id=1, source_target_pairs={{0,2},{1,3},{2,4},{3,5},{4,6},{5,7},{6,0},{7,1},{8,10},{9,11},{10,... | collective-permute-start | bytes 1179656 | tf_op jit(solution)/shard_map/ppermute | solution.py:286
  65.2 12.5 %collective-permute-start.18 = (bf16[768,256]{1,0:T(8,128)(2,1)}, bf16[768,256]{1,0:T(8,128)(2,1)}, u32[]{:S(2)}, u32[]{:S(2)}) collective-permute-start(bf16[768,256]{1,0:T(8,128)(2,1)} %slice_bitcast_fusion), channel_id=1, source_target_pairs={{0,6},{1,7},{2,0},{3,1},{4,2},{5,3},{6,4},{7,5},{8,14},{9,15},{10,... | collective-permute-start | bytes 1179656 | tf_op jit(solution)/shard_map/ppermute | solution.py:286
  75.0 15.1 %collective-permute-start.21 = (bf16[256,1280]{1,0:T(8,128)(2,1)S(1)}, bf16[256,1280]{1,0:T(8,128)(2,1)S(1)}, u32[]{:S(2)}, u32[]{:S(2)}) collective-permute-start(bf16[256,1280]{1,0:T(8,128)(2,1)S(1)} %select_dynamic-update-slice_fusion.refs_0_), channel_id=1, source_target_pairs={{0,32},{8,40},{16,48},{24,56},{32,64},{40,72},{48,80},{56,88},{64,... | collective-permute-start | bytes 1966088 | tf_op jit(solution)/shard_map/ppermute | solution.py:283
  75.0 15.1 %collective-permute-start.22 = (bf16[256,1280]{1,0:T(8,128)(2,1)S(1)}, bf16[256,1280]{1,0:T(8,128)(2,1)S(1)}, u32[]{:S(2)}, u32[]{:S(2)}) collective-permute-start(bf16[256,1280]{1,0:T(8,128)(2,1)S(1)} %select_dynamic-update-slice_fusion.refs_0_), channel_id=1, source_target_pairs={{0,224},{8,232},{16,240},{24,248},{32,0},{40,8},{48,16},{56,24},{6... | collective-permute-start | bytes 1966088 | tf_op jit(solution)/shard_map/ppermute | solution.py:283
  90.1 14.3 %collective-permute-start.23 = (bf16[256,1280]{1,0:T(8,128)(2,1)S(1)}, bf16[256,1280]{1,0:T(8,128)(2,1)}, u32[]{:S(2)}, u32[]{:S(2)}) collective-permute-start(bf16[256,1280]{1,0:T(8,128)(2,1)S(1)} %collective-permute-done.21.refs_8_), channel_id=1, source_target_pairs={{0,32},{8,40},{16,48},{24,56},{32,64},{40,72},{48,80},{56,88},{64,... | collective-permute-start | bytes 1966088 | tf_op jit(solution)/shard_map/ppermute | solution.py:283
  90.2 14.2 %collective-permute-start.24 = (bf16[256,1280]{1,0:T(8,128)(2,1)S(1)}, bf16[256,1280]{1,0:T(8,128)(2,1)}, u32[]{:S(2)}, u32[]{:S(2)}) collective-permute-start(bf16[256,1280]{1,0:T(8,128)(2,1)S(1)} %collective-permute-done.22.refs_1_), channel_id=1, source_target_pairs={{0,224},{8,232},{16,240},{24,248},{32,0},{40,8},{48,16},{56,24},{6... | collective-permute-start | bytes 1966088 | tf_op jit(solution)/shard_map/ppermute | solution.py:283
  104.4 20.8 %all-to-all-start = ((bf16[8,384,256]{2,1,0:T(8,128)(2,1)}), bf16[8,384,256]{2,1,0:T(8,128)(2,1)S(1)}, u32[]{:S(2)}, u32[]{:S(2)}) async-start(bf16[8,384,256]{2,1,0:T(8,128)(2,1)} %shard_map.132), calls=%async_computation | async-start | bytes 3145728 | tf_op jit(solution)/shard_map/all_to_all | solution.py:379
  108.0 13.7 %collective-permute-start.25 = (bf16[256,1280]{1,0:T(8,128)(2,1)}, bf16[256,1280]{1,0:T(8,128)(2,1)S(1)}, u32[]{:S(2)}, u32[]{:S(2)}) collective-permute-start(bf16[256,1280]{1,0:T(8,128)(2,1)} %collective-permute-done.23.refs_7_), channel_id=1, source_target_pairs={{0,32},{8,40},{16,48},{24,56},{32,64},{40,72},{48,80},{56,88},{64,... | collective-permute-start | bytes 1966088 | tf_op jit(solution)/shard_map/ppermute | solution.py:283
  108.5 13.3 %collective-permute-start.26 = (bf16[256,1280]{1,0:T(8,128)(2,1)}, bf16[256,1280]{1,0:T(8,128)(2,1)S(1)}, u32[]{:S(2)}, u32[]{:S(2)}) collective-permute-start(bf16[256,1280]{1,0:T(8,128)(2,1)} %collective-permute-done.24.refs_2_), channel_id=1, source_target_pairs={{0,224},{8,232},{16,240},{24,248},{32,0},{40,8},{48,16},{56,24},{6... | collective-permute-start | bytes 1966088 | tf_op jit(solution)/shard_map/ppermute | solution.py:283
  125.2 15.8 %collective-permute-start.27 = (bf16[8,384,256]{2,1,0:T(8,128)(2,1)S(1)}, bf16[8,384,256]{2,1,0:T(8,128)(2,1)S(1)}, u32[]{:S(2)}, u32[]{:S(2)}) collective-permute-start(bf16[8,384,256]{2,1,0:T(8,128)(2,1)S(1)} %all-to-all-done.own), channel_id=1, source_target_pairs={{0,8},{8,0},{16,24},{24,16},{32,40},{40,32},{48,56},{56,48},{64,72... | collective-permute-start | bytes 4718600 | tf_op jit(solution)/shard_map/ppermute | solution.py:386
  130.3 10.6 %collective-permute-start.28 = (bf16[256,640]{1,0:T(8,128)(2,1)S(1)}, bf16[256,640]{1,0:T(8,128)(2,1)S(1)}, u32[]{:S(2)}, u32[]{:S(2)}) collective-permute-start(bf16[256,640]{1,0:T(8,128)(2,1)S(1)} %slice.108), channel_id=1, source_target_pairs={{0,32},{8,40},{16,48},{24,56},{32,64},{40,72},{48,80},{56,88},{64,... | collective-permute-start | bytes 983048 | tf_op jit(solution)/shard_map/ppermute | solution.py:283
  158.5 16.1 %all-to-all-start.2 = ((bf16[16,8,768]{2,1,0:T(8,128)(2,1)}), bf16[16,8,768]{2,1,0:T(8,128)(2,1)S(1)}, u32[]{:S(2)}, u32[]{:S(2)}) async-start(bf16[16,8,768]{2,1,0:T(8,128)(2,1)} %shard_map.135), calls=%async_computation.2 | async-start | bytes 393216 | tf_op jit(solution)/shard_map/all_to_all | solution.py:410
  163.5 25.1 %collective-permute-start.30 = (bf16[384,256]{1,0:T(8,128)(2,1)}, bf16[384,256]{1,0:T(8,128)(2,1)S(1)}, u32[]{:S(2)}, u32[]{:S(2)}) collective-permute-start(bf16[384,256]{1,0:T(8,128)(2,1)} %copy-done.21), channel_id=1, source_target_pairs={{0,8},{8,0},{16,24},{24,16},{32,40},{40,32},{48,56},{56,48},{64,72... | collective-permute-start | bytes 589832 | tf_op jit(solution)/shard_map/ppermute | solution.py:396
  (43 other events, 339.6 us)
where the time goes:
time: 191 us; the launch traced here: 190 us
  waiting for transfers between devices  74.6 us (39%)
  starting transfers between devices  68.8 us (36%)
  Pallas kernels  19.3 us (10%)
  blocking collectives  15.5 us (8%)
  local copies, waits for them, and re-layouts  9.29 us (5%)
    ppermute x16, waiting for transfers between devices, z_step(): return lax.ppermute(block, 'seq', along_z(step))  32 us
    ppermute x16, starting transfers between devices, z_step(): return lax.ppermute(block, 'seq', along_z(step))  26.2 us
    pallas_call x10, Pallas kernels, call(): pl.pallas_call(body, out_shape=outs, in_specs=specs, out_specs=[VMEM] * l...  19.3 us
    all_to_all x1, waiting for transfers between devices, local(): gathered = lax.all_to_all(rows, 'seq', 0, 0, axis_index_groups=same_core)  10.4 us
    ppermute x4, waiting for transfers between devices, y_step(): return lax.ppermute(block, 'tp', along_y(step))  8.54 us
    all_to_all x1, blocking collectives, local(): summaries = lax.all_to_all(summary, 'tp', 0, 0)  7.96 us
    all_to_all x1, blocking collectives, local(): parts = lax.all_to_all(update, 'tp', 0, 0)  7.57 us
    ppermute x1, waiting for transfers between devices, local(): far = lax.ppermute(block, 'seq', XHI)  7 us
  transfers between devices with their start and end apart: 35, of which 14 were waited for; matrix products, arithmetic and copies ran while one was open for 2% of the time, Pallas kernels for 7%

commit v1 on v0

--- a/solution.py
+++ b/solution.py
@@ -60,14 +60,15 @@
 
 
 def assemble_kernel(pos, p0, p1, p2a, p2b, p3, x_out, own_sq, sib_sq):
-    core, y = pos[2], pos[3]
+    x_hi, core = pos[1], pos[2]
     rows = p0.shape[1]
     per = rows // 2
-    x_out[0:2] = p0[...]
-    x_out[2:4] = p1[...]
-    x_out[4] = p2a[...]
-    x_out[5] = p2b[...]
-    x_out[6:8] = p3[...]
+    low = x_hi == 0
+    pieces = [p0.at[0], p0.at[1], p1.at[0], p1.at[1], p2a, p2b, p3.at[0], p3.at[1]]
+    for k in range(8):
+        left, right = pieces[k][:, :128], pieces[k][:, 128:]
+        x_out[k, :, :128] = jnp.where(low, left, right)
+        x_out[k, :, 128:] = jnp.where(low, right, left)
     segs = per // SEG
     for which, ref in ((0, own_sq), (1, sib_sq)):
         base = pl.multiple_of((core if which == 0 else 1 - core) * per, per)
@@ -82,28 +83,36 @@
             )
 
 
-def project_kernel(pos, x, *refs):
-    w, (own, sib) = refs[:9], refs[9:]
+def project_kernel(pos, x, own0, far0, u1, d1, u2, d2, u3, d3, u4, d4, u5, d5, own, sib, w):
     z, core, y = pos[0], pos[2], pos[3]
-    per, width = own.shape
-    half = w[4].shape[1]
-    tile = SEG
+    per = own.shape[0]
+    w[0, 0:128, :] = own0[...]
+    w[0, 128:256, :] = far0[...]
+    w[7, 0:128, :] = u1[...]
+    w[1, 0:128, :] = d1[...]
+    w[6, 0:128, :] = u2[0:128, :]
+    w[7, 128:256, :] = u2[128:256, :]
+    w[2, 0:128, :] = d2[128:256, :]
+    w[1, 128:256, :] = d2[0:128, :]
+    w[5, 0:128, :] = u3[0:128, :]
+    w[6, 128:256, :] = u3[128:256, :]
+    w[3, 0:128, :] = d3[128:256, :]
+    w[2, 128:256, :] = d3[0:128, :]
+    w[4, 64:128, :] = u4[0:64, :]
+    w[5, 128:256, :] = u4[64:192, :]
+    w[4, 0:64, :] = d4[128:192, :]
+    w[3, 128:256, :] = d4[0:128, :]
+    w[4, 192:256, :] = u5[...]
+    w[4, 128:192, :] = d5[...]
     for which, ref in ((1, sib), (0, own)):
         base = pl.multiple_of((core if which == 0 else 1 - core) * per, per)
-        for j in range(per // tile):
-            at = pl.ds(base + j * tile, tile)
+        for j in range(per // SEG):
+            at = pl.ds(base + j * SEG, SEG)
             total = None
             for k in range(8):
-                index = lax.rem(z + k - 2 * y + 16, 8)
-                rows = x[index, at, :]
-                if k == 4:
-                    term = jnp.concatenate(
-                        [dot(rows, w[4][...]), dot(rows, w[5][:, : width - half])], axis=1
-                    )
-                else:
-                    term = dot(rows, w[k if k < 4 else k + 1][:, :width])
+                term = dot(x[lax.rem(z + k - 2 * y + 16, 8), at, :], w[k])
                 total = term if total is None else total + term
-            ref[j * tile : (j + 1) * tile, :] = total.astype(ref.dtype)
+            ref[j * SEG : (j + 1) * SEG, :] = total.astype(ref.dtype)
 
 
 def attend_kernel(valid, own, got, own_sq, got_sq, out, mixed):
@@ -297,15 +306,14 @@
     grad = jnp.sum(cotangent.astype(F32).reshape(segs, SEG, cols) * keep_rows, axis=1)
     grad = jnp.pad(grad.astype(BF), ((0, 1), (0, 0))).reshape(16, 128)
     turned = lax.ppermute(jnp.concatenate([seg_output, grad], axis=0), ("seq", "tp"), swap)
-    far, take = tie(far, take)
-
-    plane = in_order(at0, block, far, 0)
+    u1, d1 = z_step(block, 1), z_step(block, -1)
+    far, take, u1, d1 = tie(far, take, u1, d1)
+
     chip = in_order(is0, keep, take, 0)
     chip_x = lax.ppermute(chip, "tp", XLO)
-    up1, down1 = z_step(plane, 1), z_step(plane, -1)
-    up1, down1, chip_x, turned, cross_block, cross_output = tie(
-        up1, down1, chip_x, turned, cross_block, cross_output
-    )
+    up1 = z_step(jnp.concatenate([u1, far], axis=0), 1)
+    down1 = z_step(jnp.concatenate([far, d1], axis=0), -1)
+    up1, down1, chip_x = tie(up1, down1, chip_x)
 
     up2, down2 = z_step(up1, 1), z_step(down1, -1)
     p0 = in_order(low, chip[None], chip_x[None], 0)
@@ -313,20 +321,26 @@
     grad = turned[256:].reshape(segs + 1, 2, 2, 128)[:segs]
     g_keep = jnp.where(is0, grad[:, :, 0], grad[:, :, 1])
     g_take = lax.ppermute(jnp.where(is0, grad[:, :, 1], grad[:, :, 0]), "seq", CORE)
+    up2, down2, g_take, turned, cross_block, cross_output = tie(
+        up2, down2, g_take, turned, cross_block, cross_output
+    )
+
+    up3, down3 = z_step(up2[64:], 1), z_step(down2[:192], -1)
+    g_chip = jnp.concatenate(
+        [in_order(is0, g_keep, g_take, 0), jnp.zeros((8 - 2 * segs, 2, 128), BF)]
+    )
+    g_own = jnp.where(at0, g_chip[:, 0], g_chip[:, 1])
+    g_give = jnp.where(at0, g_chip[:, 1], g_chip[:, 0])
     cross_pack = jnp.concatenate(
         [cross_block, cross_output[:128], cross_output[128:], turned[:128], turned[128:256]],
         axis=1,
     )
-    cross_far = lax.ppermute(cross_pack, "seq", XHI)
-    up2, down2, cross_far, g_take = tie(up2, down2, cross_far, g_take)
-
-    up3, down3 = z_step(up2, 1), z_step(down2, -1)
-    g_chip = jnp.concatenate(
-        [in_order(is0, g_keep, g_take, 0), jnp.zeros((8 - 2 * segs, 2, 128), BF)]
-    )
-    g_own = jnp.where(at0, g_chip[:, 0], g_chip[:, 1])
-    g_far = lax.ppermute(jnp.where(at0, g_chip[:, 1], g_chip[:, 0]), "seq", XHI)
-    g_rows = in_order(at0, g_own, g_far, 1).astype(F32)
+    cross_far = lax.ppermute(
+        jnp.concatenate([cross_pack, jnp.pad(g_give, ((0, 8), (0, 1152)))], axis=0), "seq", XHI
+    )
+    up3, down3, cross_far, p3, p1 = tie(up3, down3, cross_far, p3, p1)
+    g_rows = in_order(at0, g_own, cross_far[128:136, :128], 1).astype(F32)
+    cross_far = cross_far[:128]
 
     def tall(wide):
         return jnp.concatenate([wide[:, :128], wide[:, 128:]], axis=0)
@@ -339,10 +353,8 @@
         ],
         axis=1,
     )
-    up3, down3, cross_plane, g_rows = tie(up3, down3, cross_plane, g_rows)
-
-    half = plane.shape[1] // 2
-    up4, down4 = z_step(up3[:, :half], 1), z_step(down3[:, half:], -1)
+
+    up4, down4 = z_step(up3[128:], 1), z_step(down3[:64], -1)
     p2a, p2b = y_step(p3[0], 1), y_step(p1[1], -1)
     p2a, cross_plane = tie(p2a, cross_plane)
     c_up1, c_down1 = z_step(cross_plane, 1), z_step(cross_plane, -1)
@@ -358,7 +370,8 @@
     own_p, sib_p = call(
         project_kernel,
         [shape((per, 768), F32), shape((per, 768), BF)],
-        (pos, x, plane, down1, down2, down3, up4, down4, up3, up2, up1),
+        (pos, x, block, far, u1, d1, up1, down1, up2, down2, up3, down3, up4, down4),
+        scratch=[pltpu.VMEM((8, 256, 768), BF)],
         flops=2 * 768 * 768 * 2048,
         moved=8 * 2**20,
     )

time: 191 us -> 203 us (1.063)
  starting transfers between devices: 68.8 us -> 74 us
  other arithmetic: 1.31 us -> 5.53 us
  local copies, waits for them, and re-layouts: 9.29 us -> 11.7 us
    ppermute x16 -> x18, waiting for transfers between devices: 32 us -> 39.8 us  [z_step(): return lax.ppermute(block, 'seq', along_z(step))]
    ppermute x16 -> x18, starting transfers between devices: 26.2 us -> 33.5 us  [z_step(): return lax.ppermute(block, 'seq', along_z(step))]
    ppermute x1, waiting for transfers between devices: 7 us -> 0.29 us  [local(): far = lax.ppermute(block, 'seq', XHI)]
    ppermute x2 -> x1, waiting for transfers between devices: 5.05 us -> 0.01 us  [local(): lax.ppermute(jnp.concatenate([cross_pack, jnp.pad(g_give, ((0, 8), (0, 11...]
    ppermute x4, waiting for transfers between devices: 8.54 us -> 13 us  [y_step(): return lax.ppermute(block, 'tp', along_y(step))]
    ppermute x2 -> x1, starting transfers between devices: 5.02 us -> 1.89 us  [local(): lax.ppermute(jnp.concatenate([cross_pack, jnp.pad(g_give, ((0, 8), (0, 11...]
    all_to_all x1, starting transfers between devices: 4.99 us -> 7.79 us  [local(): gathered = lax.all_to_all(rows, 'seq', 0, 0, axis_index_groups=same_core)]
    select_n x6 -> x5, other arithmetic: 0.25 us -> 2.83 us  [in_order(): jnp.where(flag, mine, other)]
  transfers between devices with their start and end apart: 35 -> 36, of which waited for: 14 -> 21; matrix products, arithmetic and copies ran while one was open for 2% -> 4% of each run, Pallas kernels for 7% -> 6%
where the time goes in v1:
time: 203 us; the launch traced here: 202 us
  waiting for transfers between devices  74.9 us (37%)
  starting transfers between devices  74 us (36%)
  Pallas kernels  19 us (9%)
  blocking collectives  15.5 us (8%)
  local copies, waits for them, and re-layouts  11.7 us (6%)
  other arithmetic  5.53 us (3%)
    ppermute x18, waiting for transfers between devices, z_step(): return lax.ppermute(block, 'seq', along_z(step))  39.8 us
    ppermute x18, starting transfers between devices, z_step(): return lax.ppermute(block, 'seq', along_z(step))  33.5 us
    pallas_call x10, Pallas kernels, call(): pl.pallas_call(body, out_shape=outs, in_specs=specs, out_specs=[VMEM] * l...  19 us
    ppermute x4, waiting for transfers between devices, y_step(): return lax.ppermute(block, 'tp', along_y(step))  13 us
    all_to_all x1, waiting for transfers between devices, local(): gathered = lax.all_to_all(rows, 'seq', 0, 0, axis_index_groups=same_core)  10.4 us
    all_to_all x1, blocking collectives, local(): summaries = lax.all_to_all(summary, 'tp', 0, 0)  7.96 us
    all_to_all x1, starting transfers between devices, local(): gathered = lax.all_to_all(rows, 'seq', 0, 0, axis_index_groups=same_core)  7.79 us
    all_to_all x1, blocking collectives, local(): parts = lax.all_to_all(update, 'tp', 0, 0)  7.57 us
  transfers between devices with their start and end apart: 36, of which 21 were waited for; matrix products, arithmetic and copies ran while one was open for 4% of the time, Pallas kernels for 6%

profile of v1, /device:TPU:1, one launch (start us, length us, event | category | flops | bytes accessed | tf_op | source)
XLA Modules:
  0.0 202.0 jit_solution(7288241971755868250)
XLA Ops:
  3.2 6.4 %collective-permute-start.3 = (bf16[128,768]{1,0:T(8,128)(2,1)S(1)}, bf16[128,768]{1,0:T(8,128)(2,1)S(1)}, u32[]{:S(2)}, u32[]{:S(2)}) collective-permute-start(bf16[128,768]{1,0:T(8,128)(2,1)S(1)} %constant_dynamic-update-slice_fusion.own0), channel_id=1, source_target_pairs={{0,224},{8,232},{16,240},{24,248},{32,0},{40,8},{48,16},{56,24},{6... | collective-permute-start | bytes 589832 | tf_op jit(solution)/shard_map/ppermute | solution.py:292
  9.6 2.7 %collective-permute-start = (bf16[128,768]{1,0:T(8,128)(2,1)S(1)}, bf16[128,768]{1,0:T(8,128)(2,1)S(1)}, u32[]{:S(2)}, u32[]{:S(2)}) collective-permute-start(bf16[128,768]{1,0:T(8,128)(2,1)S(1)} %constant_dynamic-update-slice_fusion.own0), channel_id=1, source_target_pairs={{0,16},{8,24},{16,0},{24,8},{32,48},{40,56},{48,32},{56,40},{64,80... | collective-permute-start | bytes 589832 | tf_op jit(solution)/shard_map/ppermute | solution.py:302
  21.4 4.8 %collective-permute-done.6 = bf16[768,256]{1,0:T(8,128)(2,1)} collective-permute-done((bf16[768,256]{1,0:T(8,128)(2,1)S(1)}, bf16[768,256]{1,0:T(8,128)(2,1)}, u32[]{:S(2)}, u32[]{:S(2)}) %collective-permute-start.6) | collective-permute-done | bytes 393248 | tf_op jit(solution)/shard_map/ppermute | solution.py:313
  26.7 3.0 %collective-permute-done.4.u2 = bf16[256,768]{1,0:T(8,128)(2,1)} collective-permute-done((bf16[256,768]{1,0:T(8,128)(2,1)S(1)}, bf16[256,768]{1,0:T(8,128)(2,1)}, u32[]{:S(2)}, u32[]{:S(2)}) %collective-permute-start.4) | collective-permute-done | bytes 393248 | tf_op jit(solution)/shard_map/ppermute | solution.py:292
  32.2 7.9 %collective-permute-start.8 = (bf16[256,768]{1,0:T(8,128)(2,1)}, bf16[256,768]{1,0:T(8,128)(2,1)S(1)}, u32[]{:S(2)}, u32[]{:S(2)}) collective-permute-start(bf16[256,768]{1,0:T(8,128)(2,1)} %collective-permute-done.5.d2), channel_id=1, source_target_pairs={{0,224},{8,232},{16,240},{24,248},{32,0},{40,8},{48,16},{56,24},{6... | collective-permute-start | bytes 1179656 | tf_op jit(solution)/shard_map/ppermute | solution.py:292
  40.1 3.0 %collective-permute-start.10 = (bf16[3,2,128]{2,0,1:T(4,128)(2,1)S(1)}, bf16[3,2,128]{2,0,1:T(4,128)(2,1)S(1)}, u32[]{:S(2)}, u32[]{:S(2)}) collective-permute-start(bf16[3,2,128]{2,0,1:T(4,128)(2,1)S(1)} %select_bitcast_fusion.3), channel_id=1, source_target_pairs={{0,8},{8,0},{16,24},{24,16},{32,40},{40,32},{48,56},{56,48},{64,72... | collective-permute-start | bytes 4616 | tf_op jit(solution)/shard_map/ppermute | solution.py:323
  52.9 4.6 %collective-permute-done.12.d4 = bf16[192,768]{1,0:T(8,128)(2,1)} collective-permute-done((bf16[192,768]{1,0:T(8,128)(2,1)}, bf16[192,768]{1,0:T(8,128)(2,1)}, u32[]{:S(2)}, u32[]{:S(2)}) %collective-permute-start.12) | collective-permute-done | bytes 294944 | tf_op jit(solution)/shard_map/ppermute | solution.py:292
  59.3 4.3 %collective-permute-done.15.p1 = bf16[2,768,256]{2,1,0:T(8,128)(2,1)S(1)} collective-permute-done((bf16[2,768,256]{2,1,0:T(8,128)(2,1)S(1)}, bf16[2,768,256]{2,1,0:T(8,128)(2,1)S(1)}, u32[]{:S(2)}, u32[]{:S(2)}) %collective-permute-start.15) | collective-permute-done | bytes 786464 | tf_op jit(solution)/shard_map/ppermute | solution.py:295
  74.1 7.3 %collective-permute-done.18.p2a = bf16[768,256]{1,0:T(8,128)(2,1)S(1)} collective-permute-done((bf16[768,256]{1,0:T(8,128)(2,1)S(1)}, bf16[768,256]{1,0:T(8,128)(2,1)S(1)}, u32[]{:S(2)}, u32[]{:S(2)}) %collective-permute-start.18) | collective-permute-done | bytes 393248 | tf_op jit(solution)/shard_map/ppermute | solution.py:295
  81.5 3.1 %collective-permute-start.23 = (bf16[256,1280]{1,0:T(8,128)(2,1)S(1)}, bf16[256,1280]{1,0:T(8,128)(2,1)S(1)}, u32[]{:S(2)}, u32[]{:S(2)}) collective-permute-start(bf16[256,1280]{1,0:T(8,128)(2,1)S(1)} %select_dynamic-update-slice_fusion.refs_0_), channel_id=1, source_target_pairs={{0,224},{8,232},{16,240},{24,248},{32,0},{40,8},{48,16},{56,24},{6... | collective-permute-start | bytes 1966088 | tf_op jit(solution)/shard_map/ppermute | solution.py:292
  87.6 3.9 %shard_map.131 = (f32[384,768]{1,0:T(8,128)S(1)}, bf16[384,768]{1,0:T(8,128)(2,1)S(1)}) custom-call(s32[5]{0:T(128)S(1)} %stack.23.pos, bf16[8,768,256]{2,1,0:T(8,128)(2,1)S(1)} %get-tuple-element.74.x, bf16[128,768]{1,0:T(8,128)(2,1)S(1)} %copy-done.19, bf16[128,768]{1,0:T(8,128)(2,1)S(1)} %copy-done.17, bf16[128,768]{1,0:T(8,128)(2,1)S(1)} %copy-done.15, ...), custom_call_target="tpu_custom_call" | custom-call | flops 2415919104 | bytes 8388608 | tf_op jit(solution)/shard_map/pallas_call | solution.py:33
  96.3 3.1 %collective-permute-done.22.refs_8_ = bf16[256,1280]{1,0:T(8,128)(2,1)S(1)} collective-permute-done((bf16[256,1280]{1,0:T(8,128)(2,1)S(1)}, bf16[256,1280]{1,0:T(8,128)(2,1)S(1)}, u32[]{:S(2)}, u32[]{:S(2)}) %collective-permute-start.22) | collective-permute-done | bytes 655392 | tf_op jit(solution)/shard_map/ppermute | solution.py:292
  102.1 3.8 %shard_map.132 = bf16[8,384,256]{2,1,0:T(8,128)(2,1)} custom-call(s32[3]{0:T(128)S(1)} %copy-done.20, f32[384,768]{1,0:T(8,128)S(1)} %get-tuple-element.77.own, bf16[384,768]{1,0:T(8,128)(2,1)S(1)} %collective-permute-done.20.got, f32[384,128]{1,0:T(8,128)S(1)} %get-tuple-element.82.own_sq, f32[384,128]{1,0:T(8,128)S(1)} %collective-permute-done.21.got_sq), custom_call_target="tpu_custom_call" | custom-call | flops 100000000 | bytes 3145728 | tf_op jit(solution)/shard_map/pallas_call | solution.py:33
  105.9 7.5 %collective-permute-done.24.refs_7_ = bf16[256,1280]{1,0:T(8,128)(2,1)} collective-permute-done((bf16[256,1280]{1,0:T(8,128)(2,1)S(1)}, bf16[256,1280]{1,0:T(8,128)(2,1)}, u32[]{:S(2)}, u32[]{:S(2)}) %collective-permute-start.24) | collective-permute-done | bytes 655392 | tf_op jit(solution)/shard_map/ppermute | solution.py:292
  113.5 3.6 %all-to-all-start = ((bf16[8,384,256]{2,1,0:T(8,128)(2,1)}), bf16[8,384,256]{2,1,0:T(8,128)(2,1)S(1)}, u32[]{:S(2)}, u32[]{:S(2)}) async-start(bf16[8,384,256]{2,1,0:T(8,128)(2,1)} %shard_map.132), calls=%async_computation | async-start | bytes 3145728 | tf_op jit(solution)/shard_map/all_to_all | solution.py:392
  119.8 10.6 %collective-permute-done.26.refs_6_ = bf16[256,1280]{1,0:T(8,128)(2,1)S(1)} collective-permute-done((bf16[256,1280]{1,0:T(8,128)(2,1)}, bf16[256,1280]{1,0:T(8,128)(2,1)S(1)}, u32[]{:S(2)}, u32[]{:S(2)}) %collective-permute-start.26) | collective-permute-done | bytes 655392 | tf_op jit(solution)/shard_map/ppermute | solution.py:292
  130.4 3.6 %all-to-all-done.own = bf16[8,384,256]{2,1,0:T(8,128)(2,1)S(1)} async-done(((bf16[8,384,256]{2,1,0:T(8,128)(2,1)}), bf16[8,384,256]{2,1,0:T(8,128)(2,1)S(1)}, u32[]{:S(2)}, u32[]{:S(2)}) %all-to-all-start) | async-done | bytes 1572896 | tf_op jit(solution)/shard_map/all_to_all | solution.py:392
  134.0 5.3 %collective-permute-start.28 = (bf16[8,384,256]{2,1,0:T(8,128)(2,1)S(1)}, bf16[8,384,256]{2,1,0:T(8,128)(2,1)S(1)}, u32[]{:S(2)}, u32[]{:S(2)}) collective-permute-start(bf16[8,384,256]{2,1,0:T(8,128)(2,1)S(1)} %all-to-all-done.own), channel_id=1, source_target_pairs={{0,8},{8,0},{16,24},{24,16},{32,40},{40,32},{48,56},{56,48},{64,72... | collective-permute-start | bytes 4718600 | tf_op jit(solution)/shard_map/ppermute | solution.py:399
  142.9 7.2 %collective-permute-done.29.refs_4_ = bf16[256,640]{1,0:T(8,128)(2,1)S(1)} collective-permute-done((bf16[256,640]{1,0:T(8,128)(2,1)S(1)}, bf16[256,640]{1,0:T(8,128)(2,1)S(1)}, u32[]{:S(2)}, u32[]{:S(2)}) %collective-permute-start.29) | collective-permute-done | bytes 327712 | tf_op jit(solution)/shard_map/ppermute | solution.py:292
  154.1 8.0 %all_to_all.20.rows.grads = f32[8,16,256]{2,1,0:T(8,128)S(1)} all-to-all(f32[8,16,256]{2,1,0:T(8,128)S(1)} %get-tuple-element.94), channel_id=1, replica_groups=mesh['seq'=32,'tp'=8] {'tp'}, dimensions={0} | all-to-all | bytes 262144 | tf_op jit(solution)/shard_map/all_to_all | solution.py:408
  167.6 7.8 %all-to-all-start.2 = ((bf16[16,8,768]{2,1,0:T(8,128)(2,1)}), bf16[16,8,768]{2,1,0:T(8,128)(2,1)S(1)}, u32[]{:S(2)}, u32[]{:S(2)}) async-start(bf16[16,8,768]{2,1,0:T(8,128)(2,1)} %shard_map.135), calls=%async_computation.2 | async-start | bytes 393216 | tf_op jit(solution)/shard_map/all_to_all | solution.py:423
  176.1 10.4 %all-to-all-done.2.gathered = bf16[16,8,768]{2,1,0:T(8,128)(2,1)S(1)} async-done(((bf16[16,8,768]{2,1,0:T(8,128)(2,1)}), bf16[16,8,768]{2,1,0:T(8,128)(2,1)S(1)}, u32[]{:S(2)}, u32[]{:S(2)}) %all-to-all-start.2) | async-done | bytes 196640 | tf_op jit(solution)/shard_map/all_to_all | solution.py:423
  188.0 7.6 %all_to_all.21.parts = f32[8,8,256]{2,1,0:T(8,128)S(1)} all-to-all(f32[8,8,256]{2,1,0:T(8,128)S(1)} %get-tuple-element.97), channel_id=1, replica_groups=mesh['seq'=32,'tp'=8] {'tp'}, dimensions={0} | all-to-all | bytes 131072 | tf_op jit(solution)/shard_map/all_to_all | solution.py:432
  196.2 3.3 %collective-permute-start.33 = (f32[8,256]{1,0:T(8,128)S(1)}, f32[8,256]{1,0:T(8,128)S(1)}, u32[]{:S(2)}, u32[]{:S(2)}) collective-permute-start(f32[8,256]{1,0:T(8,128)S(1)} %get-tuple-element.99), channel_id=1, source_target_pairs={{0,8},{8,0},{16,24},{24,16},{32,40},{40,32},{48,56},{56,48},{64,72... | collective-permute-start | bytes 24584 | tf_op jit(solution)/shard_map/ppermute | solution.py:436
  (171 shorter events, 67.8 us)
Async XLA Ops:
  3.2 12.9 %collective-permute-start.3 = (bf16[128,768]{1,0:T(8,128)(2,1)S(1)}, bf16[128,768]{1,0:T(8,128)(2,1)S(1)}, u32[]{:S(2)}, u32[]{:S(2)}) collective-permute-start(bf16[128,768]{1,0:T(8,128)(2,1)S(1)} %constant_dynamic-update-slice_fusion.own0), channel_id=1, source_target_pairs={{0,224},{8,232},{16,240},{24,248},{32,0},{40,8},{48,16},{56,24},{6... | collective-permute-start | bytes 589832 | tf_op jit(solution)/shard_map/ppermute | solution.py:292
  16.9 9.2 %collective-permute-start.6 = (bf16[768,256]{1,0:T(8,128)(2,1)S(1)}, bf16[768,256]{1,0:T(8,128)(2,1)}, u32[]{:S(2)}, u32[]{:S(2)}) collective-permute-start(bf16[768,256]{1,0:T(8,128)(2,1)S(1)} %pad_maximum_fusion.1.chip), channel_id=1, source_target_pairs={{0,1},{1,0},{2,3},{3,2},{4,5},{5,4},{6,7},{7,6},{8,9},{9,8},{10,11... | collective-permute-start | bytes 1179656 | tf_op jit(solution)/shard_map/ppermute | solution.py:313
  20.5 9.2 %collective-permute-start.4 = (bf16[256,768]{1,0:T(8,128)(2,1)S(1)}, bf16[256,768]{1,0:T(8,128)(2,1)}, u32[]{:S(2)}, u32[]{:S(2)}) collective-permute-start(bf16[256,768]{1,0:T(8,128)(2,1)S(1)} %get-tuple-element.120), channel_id=1, source_target_pairs={{0,32},{8,40},{16,48},{24,56},{32,64},{40,72},{48,80},{56,88},{64,... | collective-permute-start | bytes 1179656 | tf_op jit(solution)/shard_map/ppermute | solution.py:292
  29.7 17.3 %collective-permute-start.7 = (bf16[256,768]{1,0:T(8,128)(2,1)}, bf16[256,768]{1,0:T(8,128)(2,1)S(1)}, u32[]{:S(2)}, u32[]{:S(2)}) collective-permute-start(bf16[256,768]{1,0:T(8,128)(2,1)} %collective-permute-done.4.u2), channel_id=1, source_target_pairs={{0,32},{8,40},{16,48},{24,56},{32,64},{40,72},{48,80},{56,88},{64,... | collective-permute-start | bytes 1179656 | tf_op jit(solution)/shard_map/ppermute | solution.py:292
  32.2 14.8 %collective-permute-start.8 = (bf16[256,768]{1,0:T(8,128)(2,1)}, bf16[256,768]{1,0:T(8,128)(2,1)S(1)}, u32[]{:S(2)}, u32[]{:S(2)}) collective-permute-start(bf16[256,768]{1,0:T(8,128)(2,1)} %collective-permute-done.5.d2), channel_id=1, source_target_pairs={{0,224},{8,232},{16,240},{24,248},{32,0},{40,8},{48,16},{56,24},{6... | collective-permute-start | bytes 1179656 | tf_op jit(solution)/shard_map/ppermute | solution.py:292
  44.3 19.3 %collective-permute-start.15 = (bf16[2,768,256]{2,1,0:T(8,128)(2,1)S(1)}, bf16[2,768,256]{2,1,0:T(8,128)(2,1)S(1)}, u32[]{:S(2)}, u32[]{:S(2)}) collective-permute-start(bf16[2,768,256]{2,1,0:T(8,128)(2,1)S(1)} %pad_maximum_fusion.p0), channel_id=1, source_target_pairs={{0,6},{1,7},{2,0},{3,1},{4,2},{5,3},{6,4},{7,5},{8,14},{9,15},{10,... | collective-permute-start | bytes 2359304 | tf_op jit(solution)/shard_map/ppermute | solution.py:295
  44.4 20.6 %collective-permute-start.14 = (bf16[2,768,256]{2,1,0:T(8,128)(2,1)S(1)}, bf16[2,768,256]{2,1,0:T(8,128)(2,1)S(1)}, u32[]{:S(2)}, u32[]{:S(2)}) collective-permute-start(bf16[2,768,256]{2,1,0:T(8,128)(2,1)S(1)} %pad_maximum_fusion.p0), channel_id=1, source_target_pairs={{0,2},{1,3},{2,4},{3,5},{4,6},{5,7},{6,0},{7,1},{8,10},{9,11},{10,... | collective-permute-start | bytes 2359304 | tf_op jit(solution)/shard_map/ppermute | solution.py:295
  47.9 11.4 %collective-permute-start.13 = (bf16[144,1280]{1,0:T(8,128)(2,1)}, bf16[144,1280]{1,0:T(8,128)(2,1)}, u32[]{:S(2)}, u32[]{:S(2)}) collective-permute-start(bf16[144,1280]{1,0:T(8,128)(2,1)} %fusion.2), channel_id=1, source_target_pairs={{0,16},{8,24},{16,0},{24,8},{32,48},{40,56},{48,32},{56,40},{64,80... | collective-permute-start | bytes 1105928 | tf_op jit(solution)/shard_map/ppermute | solution.py:338
  68.7 15.8 %collective-permute-start.17 = (bf16[64,768]{1,0:T(8,128)(2,1)S(1)}, bf16[64,768]{1,0:T(8,128)(2,1)S(1)}, u32[]{:S(2)}, u32[]{:S(2)}) collective-permute-start(bf16[64,768]{1,0:T(8,128)(2,1)S(1)} %slice.114), channel_id=1, source_target_pairs={{0,224},{8,232},{16,240},{24,248},{32,0},{40,8},{48,16},{56,24},{6... | collective-permute-start | bytes 294920 | tf_op jit(solution)/shard_map/ppermute | solution.py:292
  70.3 14.3 %collective-permute-start.16 = (bf16[64,768]{1,0:T(8,128)(2,1)S(1)}, bf16[64,768]{1,0:T(8,128)(2,1)S(1)}, u32[]{:S(2)}, u32[]{:S(2)}) collective-permute-start(bf16[64,768]{1,0:T(8,128)(2,1)S(1)} %slice.113), channel_id=1, source_target_pairs={{0,32},{8,40},{16,48},{24,56},{32,64},{40,72},{48,80},{56,88},{64,... | collective-permute-start | bytes 294920 | tf_op jit(solution)/shard_map/ppermute | solution.py:292
  71.3 10.2 %collective-permute-start.18 = (bf16[768,256]{1,0:T(8,128)(2,1)S(1)}, bf16[768,256]{1,0:T(8,128)(2,1)S(1)}, u32[]{:S(2)}, u32[]{:S(2)}) collective-permute-start(bf16[768,256]{1,0:T(8,128)(2,1)S(1)} %slice_bitcast_fusion.1), channel_id=1, source_target_pairs={{0,2},{1,3},{2,4},{3,5},{4,6},{5,7},{6,0},{7,1},{8,10},{9,11},{10,... | collective-permute-start | bytes 1179656 | tf_op jit(solution)/shard_map/ppermute | solution.py:295
  71.4 13.1 %collective-permute-start.19 = (bf16[768,256]{1,0:T(8,128)(2,1)S(1)}, bf16[768,256]{1,0:T(8,128)(2,1)S(1)}, u32[]{:S(2)}, u32[]{:S(2)}) collective-permute-start(bf16[768,256]{1,0:T(8,128)(2,1)S(1)} %slice_bitcast_fusion), channel_id=1, source_target_pairs={{0,6},{1,7},{2,0},{3,1},{4,2},{5,3},{6,4},{7,5},{8,14},{9,15},{10,... | collective-permute-start | bytes 1179656 | tf_op jit(solution)/shard_map/ppermute | solution.py:295
  81.5 14.8 %collective-permute-start.23 = (bf16[256,1280]{1,0:T(8,128)(2,1)S(1)}, bf16[256,1280]{1,0:T(8,128)(2,1)S(1)}, u32[]{:S(2)}, u32[]{:S(2)}) collective-permute-start(bf16[256,1280]{1,0:T(8,128)(2,1)S(1)} %select_dynamic-update-slice_fusion.refs_0_), channel_id=1, source_target_pairs={{0,224},{8,232},{16,240},{24,248},{32,0},{40,8},{48,16},{56,24},{6... | collective-permute-start | bytes 1966088 | tf_op jit(solution)/shard_map/ppermute | solution.py:292
  84.5 14.9 %collective-permute-start.22 = (bf16[256,1280]{1,0:T(8,128)(2,1)S(1)}, bf16[256,1280]{1,0:T(8,128)(2,1)S(1)}, u32[]{:S(2)}, u32[]{:S(2)}) collective-permute-start(bf16[256,1280]{1,0:T(8,128)(2,1)S(1)} %select_dynamic-update-slice_fusion.refs_0_), channel_id=1, source_target_pairs={{0,32},{8,40},{16,48},{24,56},{32,64},{40,72},{48,80},{56,88},{64,... | collective-permute-start | bytes 1966088 | tf_op jit(solution)/shard_map/ppermute | solution.py:292
  99.4 14.1 %collective-permute-start.24 = (bf16[256,1280]{1,0:T(8,128)(2,1)S(1)}, bf16[256,1280]{1,0:T(8,128)(2,1)}, u32[]{:S(2)}, u32[]{:S(2)}) collective-permute-start(bf16[256,1280]{1,0:T(8,128)(2,1)S(1)} %collective-permute-done.22.refs_8_), channel_id=1, source_target_pairs={{0,32},{8,40},{16,48},{24,56},{32,64},{40,72},{48,80},{56,88},{64,... | collective-permute-start | bytes 1966088 | tf_op jit(solution)/shard_map/ppermute | solution.py:292
  99.4 14.1 %collective-permute-start.25 = (bf16[256,1280]{1,0:T(8,128)(2,1)S(1)}, bf16[256,1280]{1,0:T(8,128)(2,1)}, u32[]{:S(2)}, u32[]{:S(2)}) collective-permute-start(bf16[256,1280]{1,0:T(8,128)(2,1)S(1)} %collective-permute-done.23.refs_1_), channel_id=1, source_target_pairs={{0,224},{8,232},{16,240},{24,248},{32,0},{40,8},{48,16},{56,24},{6... | collective-permute-start | bytes 1966088 | tf_op jit(solution)/shard_map/ppermute | solution.py:292
  113.5 20.6 %all-to-all-start = ((bf16[8,384,256]{2,1,0:T(8,128)(2,1)}), bf16[8,384,256]{2,1,0:T(8,128)(2,1)S(1)}, u32[]{:S(2)}, u32[]{:S(2)}) async-start(bf16[8,384,256]{2,1,0:T(8,128)(2,1)} %shard_map.132), calls=%async_computation | async-start | bytes 3145728 | tf_op jit(solution)/shard_map/all_to_all | solution.py:392
  117.1 13.3 %collective-permute-start.26 = (bf16[256,1280]{1,0:T(8,128)(2,1)}, bf16[256,1280]{1,0:T(8,128)(2,1)S(1)}, u32[]{:S(2)}, u32[]{:S(2)}) collective-permute-start(bf16[256,1280]{1,0:T(8,128)(2,1)} %collective-permute-done.24.refs_7_), channel_id=1, source_target_pairs={{0,32},{8,40},{16,48},{24,56},{32,64},{40,72},{48,80},{56,88},{64,... | collective-permute-start | bytes 1966088 | tf_op jit(solution)/shard_map/ppermute | solution.py:292
  117.2 13.2 %collective-permute-start.27 = (bf16[256,1280]{1,0:T(8,128)(2,1)}, bf16[256,1280]{1,0:T(8,128)(2,1)S(1)}, u32[]{:S(2)}, u32[]{:S(2)}) collective-permute-start(bf16[256,1280]{1,0:T(8,128)(2,1)} %collective-permute-done.25.refs_2_), channel_id=1, source_target_pairs={{0,224},{8,232},{16,240},{24,248},{32,0},{40,8},{48,16},{56,24},{6... | collective-permute-start | bytes 1966088 | tf_op jit(solution)/shard_map/ppermute | solution.py:292
  134.0 16.0 %collective-permute-start.28 = (bf16[8,384,256]{2,1,0:T(8,128)(2,1)S(1)}, bf16[8,384,256]{2,1,0:T(8,128)(2,1)S(1)}, u32[]{:S(2)}, u32[]{:S(2)}) collective-permute-start(bf16[8,384,256]{2,1,0:T(8,128)(2,1)S(1)} %all-to-all-done.own), channel_id=1, source_target_pairs={{0,8},{8,0},{16,24},{24,16},{32,40},{40,32},{48,56},{56,48},{64,72... | collective-permute-start | bytes 4718600 | tf_op jit(solution)/shard_map/ppermute | solution.py:399
  139.4 10.6 %collective-permute-start.29 = (bf16[256,640]{1,0:T(8,128)(2,1)S(1)}, bf16[256,640]{1,0:T(8,128)(2,1)S(1)}, u32[]{:S(2)}, u32[]{:S(2)}) collective-permute-start(bf16[256,640]{1,0:T(8,128)(2,1)S(1)} %slice.124), channel_id=1, source_target_pairs={{0,32},{8,40},{16,48},{24,56},{32,64},{40,72},{48,80},{56,88},{64,... | collective-permute-start | bytes 983048 | tf_op jit(solution)/shard_map/ppermute | solution.py:292
  139.5 10.5 %collective-permute-start.30 = (bf16[256,640]{1,0:T(8,128)(2,1)S(1)}, bf16[256,640]{1,0:T(8,128)(2,1)S(1)}, u32[]{:S(2)}, u32[]{:S(2)}) collective-permute-start(bf16[256,640]{1,0:T(8,128)(2,1)S(1)} %slice.125), channel_id=1, source_target_pairs={{0,224},{8,232},{16,240},{24,248},{32,0},{40,8},{48,16},{56,24},{6... | collective-permute-start | bytes 983048 | tf_op jit(solution)/shard_map/ppermute | solution.py:292
  167.6 18.9 %all-to-all-start.2 = ((bf16[16,8,768]{2,1,0:T(8,128)(2,1)}), bf16[16,8,768]{2,1,0:T(8,128)(2,1)S(1)}, u32[]{:S(2)}, u32[]{:S(2)}) async-start(bf16[16,8,768]{2,1,0:T(8,128)(2,1)} %shard_map.135), calls=%async_computation.2 | async-start | bytes 393216 | tf_op jit(solution)/shard_map/all_to_all | solution.py:423
  175.4 25.1 %collective-permute-start.31 = (bf16[384,256]{1,0:T(8,128)(2,1)}, bf16[384,256]{1,0:T(8,128)(2,1)S(1)}, u32[]{:S(2)}, u32[]{:S(2)}) collective-permute-start(bf16[384,256]{1,0:T(8,128)(2,1)} %copy-done.21), channel_id=1, source_target_pairs={{0,8},{8,0},{16,24},{24,16},{32,40},{40,32},{48,56},{56,48},{64,72... | collective-permute-start | bytes 589832 | tf_op jit(solution)/shard_map/ppermute | solution.py:409
  (42 other events, 320.2 us)
